TPU v7x, 32 devices: a whole 2x2x4 slice. The times are simulated.
32 devices in a mesh: ctx: 8 (over z, x), tp: 4 (over y, core).
Axes of the slice: x: 2, y: 2, z: 4, core: 2. Of those that a mesh axis runs over, the one named last changes fastest.
Arguments:
- query_in: bfloat16 [4096, 4096], P('ctx', 'tp'), may hold values from -6 to 6
- key_in: bfloat16 [4096, 4096], P('ctx', 'tp'), may hold values from -6 to 6
- value_in: bfloat16 [4096, 4096], P('ctx', 'tp'), may hold values from -6 to 6
- out_grad: bfloat16 [4096, 4096], P('ctx', 'tp'), may hold values from -6 to 6
- doc_ids: int32 [4096], replicated, may hold values from 0 to 3, never falling along the last dimension, each value on 1 to 2048 neighbouring positions
- skip_gain: float32 [4096], P('tp'), may hold values from -4 to 4
- filter_taps: bfloat16 [2048, 8], P(('ctx', 'tp')), may hold values from -0.125 to 0.125
Outputs:
- mixed_out: bfloat16 [4096, 4096], P('ctx', 'tp')
- query_grad: bfloat16 [4096, 4096], P('ctx', 'tp')
- key_grad: bfloat16 [4096, 4096], P('ctx', 'tp')
- value_grad: bfloat16 [4096, 4096], P('ctx', 'tp')
- filter_grad: float32 [2048, 8], P(('ctx', 'tp'))
Inputs may be any that keep to these rules, and one draw needn't show every extreme that they name: `doc_ids`: ids never fall along the tokens; each document is 1 to 2048 tokens long and one is exactly 2048 long.
All inputs are finite; a program needn't handle non-finite values.
Results may differ from a plain program's by a relative error of at most 0.0049.
Values may be sent and summed in bfloat16 or wider, within the bound.
A program may use at most 128 MiB of HBM per device.

v0:
```python
import functools
import math

import jax
import jax.numpy as jnp
from jax import lax
from jax.experimental import pallas as pl
from jax.experimental.pallas import tpu as pltpu
from jax.sharding import PartitionSpec as P

FGROUP = 512
FLEN = 2048
C = 256
BAND = FLEN + C


def band_rows(first):
    wide = jnp.broadcast_to(first, (C, BAND))
    return pltpu.roll(wide, 0, 1, stride=1, stride_axis=0)


def left_diagonals(product):
    total = product[0:8]
    for q in range(1, C // 8):
        total = total + pltpu.roll(product[8 * q : 8 * q + 8], BAND - 8 * q, 1)
    row = lax.broadcasted_iota(jnp.int32, (8, BAND), 0)
    for bit in (1, 2, 4):
        total = jnp.where((row & bit) != 0, pltpu.roll(total, BAND - bit, 1), total)
    return jnp.sum(total, axis=0, keepdims=True)


def conv_kernel(taps_fwd, taps_back, ids_col, ids_src, ids_grd, src, grd, conv, back, diag, acc, wide_f, wide_b):
    rows = conv.shape[0]
    wide_f[...] = band_rows(taps_fwd[...])
    wide_b[...] = band_rows(taps_back[...])
    acc[...] = jnp.zeros_like(acc)

    def stretch(i, carry):
        at = pl.multiple_of(i * C, C)
        ids = ids_col[pl.ds(at, C), :]
        span = pl.ds(at, BAND)
        mask = ids == ids_src[:, span]
        source = src[span, :]
        grad = grd[span, :]
        w = jnp.where(mask, wide_f[...], 0.0).astype(jnp.bfloat16)
        conv[pl.ds(at, C), :] = jnp.dot(w, source, preferred_element_type=jnp.float32).astype(conv.dtype)
        own = grd[pl.ds(at, C), :]
        prod = lax.dot_general(own, source, (((1,), (1,)), ((), ())), preferred_element_type=jnp.float32)
        acc[...] += jnp.where(mask, prod, 0.0)
        w = jnp.where(ids == ids_grd[:, span], wide_b[...], 0.0).astype(jnp.bfloat16)
        back[pl.ds(at, C), :] = jnp.dot(w, grad, preferred_element_type=jnp.float32).astype(back.dtype)
        return carry

    lax.fori_loop(0, rows // C, stretch, 0)
    diag[...] = left_diagonals(acc[...])


def shift_pairs(value, steps):
    count = lax.axis_size("ctx")
    pairs = [(s, s + 2 * steps) for s in range(count) if 0 <= s + 2 * steps < count]
    return lax.ppermute(value, "ctx", pairs)


def shards(query_in, key_in, value_in, out_grad, doc_ids, skip_gain, filter_taps):
    rows, width = query_in.shape
    half = width // 2
    count = lax.axis_size("ctx")
    tps = lax.axis_size("tp")
    here = lax.axis_index("ctx")
    x = here % 2
    pair = here // 2
    big = 2 * rows
    own_taps = filter_taps.shape[0]
    swap = [(s, s ^ 1) for s in range(count)]

    groups = filter_taps.shape[1]
    shared = 2 * tps // groups
    grouped = jnp.repeat(filter_taps.T, shared, axis=0).reshape(1, tps, 2, own_taps).transpose(0, 2, 1, 3)
    grouped = jnp.broadcast_to(grouped, (count // 2, 2, tps, own_taps))
    taps = lax.all_to_all(grouped.reshape(count * tps, own_taps), ("ctx", "tp"), 0, 0, tiled=True)
    taps = taps.reshape(1, FLEN).astype(jnp.float32)
    taps_back = jnp.concatenate([taps, jnp.zeros((1, C), jnp.float32)], axis=1)
    taps_fwd = jnp.concatenate([jnp.zeros((1, 1), jnp.float32), taps[:, ::-1], jnp.zeros((1, C - 1), jnp.float32)], axis=1)

    mixed = (key_in.astype(jnp.float32) * value_in.astype(jnp.float32)).astype(jnp.bfloat16)
    cgrad = (out_grad.astype(jnp.float32) * query_in.astype(jnp.float32)).astype(jnp.bfloat16)
    low = x == 0

    def halves(a):
        keep = jnp.where(low, a[:, :half], a[:, half:])
        give = jnp.where(low, a[:, half:], a[:, :half])
        return keep, give

    def join(keep, got):
        return jnp.where(low, jnp.concatenate([keep, got]), jnp.concatenate([got, keep]))

    mk, mg = halves(mixed)
    gk, gg = halves(cgrad)
    m0 = join(mk, lax.ppermute(mg, "ctx", swap))
    g0 = join(gk, lax.ppermute(gg, "ctx", swap))
    m1 = shift_pairs(m0, 1)
    g1 = shift_pairs(g0, -1)
    m2 = shift_pairs(m1, 1)
    g2 = shift_pairs(g1, -1)
    src = jnp.concatenate([m2, m1, m0])
    grd = jnp.concatenate([g0, g1, g2])

    none = jnp.full((2 * big,), -1, jnp.int32)
    ids = jnp.concatenate([none, doc_ids, none])
    near = lax.dynamic_slice_in_dim(ids, pair * big, 5 * big)
    ids_src = near[: 3 * big].reshape(1, -1)
    ids_grd = near[2 * big :].reshape(1, -1)
    ids_col = near[2 * big : 3 * big].reshape(-1, 1)

    conv, back, diag = pl.pallas_call(
        conv_kernel,
        out_shape=(
            jax.ShapeDtypeStruct((big, half), jnp.bfloat16),
            jax.ShapeDtypeStruct((big, half), jnp.bfloat16),
            jax.ShapeDtypeStruct((1, BAND), jnp.float32),
        ),
        scratch_shapes=[pltpu.VMEM((C, BAND), jnp.float32)] * 3,
        compiler_params=pltpu.CompilerParams(vmem_limit_bytes=56 * 1024 * 1024),
    )(taps_fwd, taps_back, ids_col, ids_src, ids_grd, src, grd)

    lag_sums = diag[:, 1 : FLEN + 1][:, ::-1].reshape(count * tps, own_taps)
    pieces = lax.all_to_all(lag_sums, ("ctx", "tp"), 0, 0, tiled=True)
    scale = 1.0 / math.sqrt(FGROUP * count * rows)
    summed = pieces.reshape(count // 2, 2, tps, own_taps).sum(0) * scale
    filter_grad = summed.transpose(2, 1, 0).reshape(own_taps, groups, shared).sum(2)

    def restore(a):
        keep = jnp.where(low, a[:rows], a[rows:])
        give = jnp.where(low, a[rows:], a[:rows])
        got = lax.ppermute(give, "ctx", swap)
        return jnp.where(low, jnp.concatenate([keep, got], axis=1), jnp.concatenate([got, keep], axis=1)).astype(jnp.float32)

    f32 = lambda a: a.astype(jnp.float32)
    skip = skip_gain[None, :]
    conv = skip * f32(mixed) + restore(conv)
    mgrad = skip * f32(cgrad) + restore(back)
    return (
        (f32(query_in) * conv).astype(jnp.bfloat16),
        (f32(out_grad) * conv).astype(jnp.bfloat16),
        (mgrad * f32(value_in)).astype(jnp.bfloat16),
        (mgrad * f32(key_in)).astype(jnp.bfloat16),
        filter_grad,
    )


def solution(mesh):
    in_specs = (
        P("ctx", "tp"),
        P("ctx", "tp"),
        P("ctx", "tp"),
        P("ctx", "tp"),
        P(),
        P("tp"),
        P(("ctx", "tp"), None),
    )
    out_specs = (
        P("ctx", "tp"),
        P("ctx", "tp"),
        P("ctx", "tp"),
        P("ctx", "tp"),
        P(("ctx", "tp"), None),
    )
    return jax.shard_map(shards, mesh=mesh, in_specs=in_specs, out_specs=out_specs, check_vma=False)
```

profile of v0, /device:TPU:0, one launch (start us, length us, event | category | flops | bytes accessed | tf_op | source)
XLA Modules:
  0.0 137.7 jit_solution(4752156114173398628)
XLA Ops:
  0.7 2.1 %fusion.4 = bf16[512,1024]{1,0:T(8,128)(2,1)S(1)} fusion(bf16[512,1024]{1,0:T(8,128)(2,1)} %param.7, bf16[512,1024]{1,0:T(8,128)(2,1)} %param.10), kind=kLoop, calls=%fused_computation.12 | loop fusion | flops 2097152 | bytes 3145728 | tf_op jit(solution)/shard_map/convert_element_type | solution.py:86
  2.8 3.0 %collective-permute-start.3 = (bf16[512,512]{1,0:T(8,128)(2,1)S(1)}, bf16[512,512]{1,0:T(8,128)(2,1)S(1)}, u32[]{:S(2)}, u32[]{:S(2)}) collective-permute-start(bf16[512,512]{1,0:T(8,128)(2,1)S(1)} %get-tuple-element.20), channel_id=1, source_target_pairs={{0,4},{4,0},{8,12},{12,8},{16,20},{20,16},{24,28},{28,24},{1,5},{5... | collective-permute-start | bytes 1572872 | tf_op jit(solution)/shard_map/ppermute | solution.py:100
  6.4 12.2 %collective-permute-done.3 = bf16[512,512]{1,0:T(8,128)(2,1)S(1)} collective-permute-done((bf16[512,512]{1,0:T(8,128)(2,1)S(1)}, bf16[512,512]{1,0:T(8,128)(2,1)S(1)}, u32[]{:S(2)}, u32[]{:S(2)}) %collective-permute-start.3) | collective-permute-done | bytes 524320 | tf_op jit(solution)/shard_map/ppermute | solution.py:100
  21.3 7.7 %collective-permute-done = bf16[512,512]{1,0:T(8,128)(2,1)S(1)} collective-permute-done((bf16[512,512]{1,0:T(8,128)(2,1)S(1)}, bf16[512,512]{1,0:T(8,128)(2,1)S(1)}, u32[]{:S(2)}, u32[]{:S(2)}) %collective-permute-start) | collective-permute-done | bytes 524320 | tf_op jit(solution)/shard_map/ppermute | solution.py:99
  29.5 4.7 %collective-permute-start.1 = (bf16[1024,512]{1,0:T(8,128)(2,1)S(1)}, bf16[1024,512]{1,0:T(8,128)(2,1)}, u32[]{:S(2)}, u32[]{:S(2)}) collective-permute-start(bf16[1024,512]{1,0:T(8,128)(2,1)S(1)} %maximum_select_fusion), channel_id=1, source_target_pairs={{0,8},{4,12},{8,16},{12,20},{16,24},{20,28},{1,9},{5,13},{9,17},{1... | collective-permute-start | bytes 3145736 | tf_op jit(solution)/shard_map/ppermute | solution.py:61
  34.2 11.4 %collective-permute-done.4 = bf16[1024,512]{1,0:T(8,128)(2,1)} collective-permute-done((bf16[1024,512]{1,0:T(8,128)(2,1)S(1)}, bf16[1024,512]{1,0:T(8,128)(2,1)}, u32[]{:S(2)}, u32[]{:S(2)}) %collective-permute-start.4) | collective-permute-done | bytes 1048608 | tf_op jit(solution)/shard_map/ppermute | solution.py:61
  46.8 8.0 %collective-permute-done.1 = bf16[1024,512]{1,0:T(8,128)(2,1)} collective-permute-done((bf16[1024,512]{1,0:T(8,128)(2,1)S(1)}, bf16[1024,512]{1,0:T(8,128)(2,1)}, u32[]{:S(2)}, u32[]{:S(2)}) %collective-permute-start.1) | collective-permute-done | bytes 1048608 | tf_op jit(solution)/shard_map/ppermute | solution.py:61
  54.9 5.5 %collective-permute-start.2 = (bf16[1024,512]{1,0:T(8,128)(2,1)}, bf16[1024,512]{1,0:T(8,128)(2,1)}, u32[]{:S(2)}, u32[]{:S(2)}) collective-permute-start(bf16[1024,512]{1,0:T(8,128)(2,1)} %collective-permute-done.1), channel_id=1, source_target_pairs={{0,8},{4,12},{8,16},{12,20},{16,24},{20,28},{1,9},{5,13},{9,17},{1... | collective-permute-start | bytes 3145736 | tf_op jit(solution)/shard_map/ppermute | solution.py:61
  61.0 3.7 %all-to-all-start = ((bf16[32,1,64]{2,1,0:T(2,128)(2,1)}), bf16[32,1,64]{2,1,0:T(2,128)(2,1)S(1)}, u32[]{:S(2)}, u32[]{:S(2)}) async-start(bf16[32,1,64]{2,1,0:T(2,128)(2,1)} %copy.19), calls=%async_computation | async-start | bytes 32768 | tf_op jit(solution)/shard_map/all_to_all | solution.py:80
  66.4 14.1 %all-to-all-done = bf16[32,1,64]{2,1,0:T(2,128)(2,1)S(1)} async-done(((bf16[32,1,64]{2,1,0:T(2,128)(2,1)}), bf16[32,1,64]{2,1,0:T(2,128)(2,1)S(1)}, u32[]{:S(2)}, u32[]{:S(2)}) %all-to-all-start) | async-done | bytes 4128 | tf_op jit(solution)/shard_map/all_to_all | solution.py:80
  80.7 1.4 %rev.6 = f32[1,2048]{1,0:T(1,128)S(1)} reverse(f32[1,2048]{1,0:T(1,128)S(1)} %reshape.55), dimensions={1} | reverse | bytes 16384 | tf_op jit(solution)/shard_map/rev | solution.py:83
  83.4 3.2 %pad_maximum_fusion.1.grd = bf16[3072,512]{1,0:T(8,128)(2,1)} fusion(bf16[1024,512]{1,0:T(8,128)(2,1)} %collective-permute-done.5, bf16[1024,512]{1,0:T(8,128)(2,1)} %collective-permute-done.4, bf16[1024,512]{1,0:T(8,128)(2,1)} %copy-done.4), kind=kLoop, calls=%fused_computation.1 | loop fusion | flops 9437184 | bytes 6291456 | tf_op jit(solution)/shard_map/concatenate | solution.py:106
  86.6 3.0 %pad_maximum_fusion.src = bf16[3072,512]{1,0:T(8,128)(2,1)} fusion(bf16[1024,512]{1,0:T(8,128)(2,1)S(1)} %copy-done.6, bf16[1024,512]{1,0:T(8,128)(2,1)} %collective-permute-done.1, bf16[1024,512]{1,0:T(8,128)(2,1)} %collective-permute-done.2), kind=kLoop, calls=%fused_computation | loop fusion | flops 9437184 | bytes 6291456 | tf_op jit(solution)/shard_map/concatenate | solution.py:105
  89.6 14.0 %shard_map.110 = (bf16[1024,512]{1,0:T(8,128)(2,1)}, bf16[1024,512]{1,0:T(8,128)(2,1)}, f32[1,2304]{1,0:T(1,128)}) custom-call(f32[1,2304]{1,0:T(1,128)} %concatenate.39.taps_fwd, f32[1,2304]{1,0:T(1,128)} %concatenate.40.taps_back, s32[1024,1]{1,0:T(8,128)} %copy.20.ids_col, s32[1,3072]{1,0:T(1,128)} %bitcast.18, s32[1,3072]{1,0:T(1,128)} %bitcast.17, ...), custom_call_target="tpu_custom_call" | custom-call | tf_op jit(solution)/shard_map/pallas_call | solution.py:115
  103.7 2.3 %broadcast_select_fusion = (bf16[512,512]{1,0:T(8,128)(2,1)}, bf16[512,512]{1,0:T(8,128)(2,1)}) fusion(pred[]{:T(512)S(6)} %eq.5, bf16[1024,512]{1,0:T(8,128)(2,1)} %get-tuple-element.9), kind=kLoop, calls=%fused_computation.20 | loop fusion | flops 524288 | bytes 2097153 | tf_op jit(solution)/shard_map/jit(_where)/select_n | solution.py:134
  106.0 1.5 %collective-permute-start.7 = (bf16[512,512]{1,0:T(8,128)(2,1)}, bf16[512,512]{1,0:T(8,128)(2,1)}, u32[]{:S(2)}, u32[]{:S(2)}) collective-permute-start(bf16[512,512]{1,0:T(8,128)(2,1)} %get-tuple-element.15), channel_id=1, source_target_pairs={{0,4},{4,0},{8,12},{12,8},{16,20},{20,16},{24,28},{28,24},{1,5},{5... | collective-permute-start | bytes 1572872 | tf_op jit(solution)/shard_map/ppermute | solution.py:135
  107.5 1.4 %rev.7 = f32[1,2048]{1,0:T(1,128)S(1)} reverse(f32[1,2048]{1,0:T(1,128)S(1)} %slice.55), dimensions={1} | reverse | bytes 16384 | tf_op jit(solution)/shard_map/rev | solution.py:126
  110.8 6.6 %all-to-all-start.1 = ((f32[32,1,64]{2,1,0:T(1,128)}), f32[32,1,64]{2,1,0:T(1,128)S(1)}, u32[]{:S(2)}, u32[]{:S(2)}) async-start(f32[32,1,64]{2,1,0:T(1,128)} %bitcast.8), calls=%async_computation.1 | async-start | bytes 32768 | tf_op jit(solution)/shard_map/all_to_all | solution.py:127
  117.4 2.2 %broadcast_select_fusion.2 = (bf16[512,512]{1,0:T(8,128)(2,1)}, bf16[512,512]{1,0:T(8,128)(2,1)}) fusion(pred[]{:T(512)S(6)} %eq.5, bf16[1024,512]{1,0:T(8,128)(2,1)} %get-tuple-element.8), kind=kLoop, calls=%fused_computation.22 | loop fusion | flops 524288 | bytes 2097153 | tf_op jit(solution)/shard_map/jit(_where)/select_n | solution.py:134
  119.7 1.8 %collective-permute-start.6 = (bf16[512,512]{1,0:T(8,128)(2,1)}, bf16[512,512]{1,0:T(8,128)(2,1)}, u32[]{:S(2)}, u32[]{:S(2)}) collective-permute-start(bf16[512,512]{1,0:T(8,128)(2,1)} %get-tuple-element.17), channel_id=1, source_target_pairs={{0,4},{4,0},{8,12},{12,8},{16,20},{20,16},{24,28},{28,24},{1,5},{5... | collective-permute-start | bytes 1572872 | tf_op jit(solution)/shard_map/ppermute | solution.py:135
  121.4 3.1 %all-to-all-done.1 = f32[32,1,64]{2,1,0:T(1,128)S(1)} async-done(((f32[32,1,64]{2,1,0:T(1,128)}), f32[32,1,64]{2,1,0:T(1,128)S(1)}, u32[]{:S(2)}, u32[]{:S(2)}) %all-to-all-start.1) | async-done | bytes 8224 | tf_op jit(solution)/shard_map/all_to_all | solution.py:127
  125.1 4.5 %fusion.1 = (bf16[512,1024]{1,0:T(8,128)(2,1)}, bf16[512,1024]{1,0:T(8,128)(2,1)}) fusion(bf16[512,1024]{1,0:T(8,128)(2,1)} %param.8, bf16[512,1024]{1,0:T(8,128)(2,1)S(1)} %fusion.4, f32[1024]{0:T(1024)S(1)} %copy-done.9, bf16[512,512]{1,0:T(8,128)(2,1)} %get-tuple-element.16, bf16[512,512]{1,0:T(8,128)(2,1)} %collective-permute-done.7, pred[]{:T(512)S(6)} %eq.5, ...), kind=kLoop, calls=%fused_computation.9 | loop fusion | flops 9961472 | bytes 6295553 | tf_op jit(solution)/shard_map/convert_element_type | solution.py:146
  129.6 4.5 %collective-permute-done.6 = bf16[512,512]{1,0:T(8,128)(2,1)} collective-permute-done((bf16[512,512]{1,0:T(8,128)(2,1)}, bf16[512,512]{1,0:T(8,128)(2,1)}, u32[]{:S(2)}, u32[]{:S(2)}) %collective-permute-start.6) | collective-permute-done | bytes 524320 | tf_op jit(solution)/shard_map/ppermute | solution.py:135
  134.1 3.6 %fusion.5 = (bf16[512,1024]{1,0:T(8,128)(2,1)}, bf16[512,1024]{1,0:T(8,128)(2,1)}) fusion(bf16[512,1024]{1,0:T(8,128)(2,1)S(1)} %copy-done.2, bf16[512,1024]{1,0:T(8,128)(2,1)S(1)} %fusion.2, f32[1024]{0:T(1024)S(1)} %copy-done.9, bf16[512,512]{1,0:T(8,128)(2,1)S(1)} %copy-done.7, bf16[512,512]{1,0:T(8,128)(2,1)} %collective-permute-done.6, pred[]{:T(512)S(6)} %eq.5, ...), kind=kLoop, calls=%fused_computation.13 | loop fusion | flops 9961472 | bytes 6295553 | tf_op jit(solution)/shard_map/convert_element_type | solution.py:144
  (55 shorter events, 11.4 us)
Async XLA Ops:
  0.6 5.2 %copy-start = (bf16[512,1024]{1,0:T(8,128)(2,1)S(1)}, bf16[512,1024]{1,0:T(8,128)(2,1)}, u32[]{:S(2)}) copy-start(bf16[512,1024]{1,0:T(8,128)(2,1)} %param.9) | copy-start | bytes 3145732
  0.7 5.2 %copy-start.1 = (bf16[512,1024]{1,0:T(8,128)(2,1)S(1)}, bf16[512,1024]{1,0:T(8,128)(2,1)}, u32[]{:S(2)}) copy-start(bf16[512,1024]{1,0:T(8,128)(2,1)} %param.8) | copy-start | bytes 3145732
  2.8 15.8 %collective-permute-start.3 = (bf16[512,512]{1,0:T(8,128)(2,1)S(1)}, bf16[512,512]{1,0:T(8,128)(2,1)S(1)}, u32[]{:S(2)}, u32[]{:S(2)}) collective-permute-start(bf16[512,512]{1,0:T(8,128)(2,1)S(1)} %get-tuple-element.20), channel_id=1, source_target_pairs={{0,4},{4,0},{8,12},{12,8},{16,20},{20,16},{24,28},{28,24},{1,5},{5... | collective-permute-start | bytes 1572872 | tf_op jit(solution)/shard_map/ppermute | solution.py:100
  6.3 22.7 %collective-permute-start = (bf16[512,512]{1,0:T(8,128)(2,1)S(1)}, bf16[512,512]{1,0:T(8,128)(2,1)S(1)}, u32[]{:S(2)}, u32[]{:S(2)}) collective-permute-start(bf16[512,512]{1,0:T(8,128)(2,1)S(1)} %get-tuple-element.22), channel_id=1, source_target_pairs={{0,4},{4,0},{8,12},{12,8},{16,20},{20,16},{24,28},{28,24},{1,5},{5... | collective-permute-start | bytes 1572872 | tf_op jit(solution)/shard_map/ppermute | solution.py:99
  18.6 41.8 %copy-start.11 = (bf16[64,8]{0,1:T(8,128)(2,1)S(1)}, bf16[64,8]{0,1:T(8,128)(2,1)}, u32[]{:S(2)}) copy-start(bf16[64,8]{0,1:T(8,128)(2,1)} %param.13) | copy-start | bytes 3076
  18.6 46.2 %copy-start.8 = (s32[4096]{0:T(1024)S(1)}, s32[4096]{0:T(1024)}, u32[]{:S(2)}) copy-start(s32[4096]{0:T(1024)} %param.11) | copy-start | bytes 49156
  19.1 1.0 copy-start.4
  20.0 25.5 %collective-permute-start.4 = (bf16[1024,512]{1,0:T(8,128)(2,1)S(1)}, bf16[1024,512]{1,0:T(8,128)(2,1)}, u32[]{:S(2)}, u32[]{:S(2)}) collective-permute-start(bf16[1024,512]{1,0:T(8,128)(2,1)S(1)} %maximum_select_fusion.1), channel_id=1, source_target_pairs={{8,0},{12,4},{16,8},{20,12},{24,16},{28,20},{9,1},{13,5},{17,9},{2... | collective-permute-start | bytes 3145736 | tf_op jit(solution)/shard_map/ppermute | solution.py:61
  29.5 16.1 %copy-start.5 = (bf16[1024,512]{1,0:T(8,128)(2,1)}, bf16[1024,512]{1,0:T(8,128)(2,1)S(1)}, u32[]{:S(2)}) copy-start(bf16[1024,512]{1,0:T(8,128)(2,1)S(1)} %maximum_select_fusion) | copy-start | bytes 3145732
  29.5 25.4 %collective-permute-start.1 = (bf16[1024,512]{1,0:T(8,128)(2,1)S(1)}, bf16[1024,512]{1,0:T(8,128)(2,1)}, u32[]{:S(2)}, u32[]{:S(2)}) collective-permute-start(bf16[1024,512]{1,0:T(8,128)(2,1)S(1)} %maximum_select_fusion), channel_id=1, source_target_pairs={{0,8},{4,12},{8,16},{12,20},{16,24},{20,28},{1,9},{5,13},{9,17},{1... | collective-permute-start | bytes 3145736 | tf_op jit(solution)/shard_map/ppermute | solution.py:61
  45.5 37.9 %collective-permute-start.5 = (bf16[1024,512]{1,0:T(8,128)(2,1)}, bf16[1024,512]{1,0:T(8,128)(2,1)}, u32[]{:S(2)}, u32[]{:S(2)}) collective-permute-start(bf16[1024,512]{1,0:T(8,128)(2,1)} %collective-permute-done.4), channel_id=1, source_target_pairs={{8,0},{12,4},{16,8},{20,12},{24,16},{28,20},{9,1},{13,5},{17,9},{2... | collective-permute-start | bytes 3145736 | tf_op jit(solution)/shard_map/ppermute | solution.py:61
  54.9 31.8 %collective-permute-start.2 = (bf16[1024,512]{1,0:T(8,128)(2,1)}, bf16[1024,512]{1,0:T(8,128)(2,1)}, u32[]{:S(2)}, u32[]{:S(2)}) collective-permute-start(bf16[1024,512]{1,0:T(8,128)(2,1)} %collective-permute-done.1), channel_id=1, source_target_pairs={{0,8},{4,12},{8,16},{12,20},{16,24},{20,28},{1,9},{5,13},{9,17},{1... | collective-permute-start | bytes 3145736 | tf_op jit(solution)/shard_map/ppermute | solution.py:61
  61.0 19.5 %all-to-all-start = ((bf16[32,1,64]{2,1,0:T(2,128)(2,1)}), bf16[32,1,64]{2,1,0:T(2,128)(2,1)S(1)}, u32[]{:S(2)}, u32[]{:S(2)}) async-start(bf16[32,1,64]{2,1,0:T(2,128)(2,1)} %copy.19), calls=%async_computation | async-start | bytes 32768 | tf_op jit(solution)/shard_map/all_to_all | solution.py:80
  83.4 3.2 %copy-start.6 = (bf16[1024,512]{1,0:T(8,128)(2,1)S(1)}, bf16[1024,512]{1,0:T(8,128)(2,1)}, u32[]{:S(2)}) copy-start(bf16[1024,512]{1,0:T(8,128)(2,1)} %copy-done.5) | copy-start | bytes 3145732
  103.7 3.8 %copy-start.10 = (f32[1,2304]{1,0:T(1,128)S(1)}, f32[1,2304]{1,0:T(1,128)}, u32[]{:S(2)}) copy-start(f32[1,2304]{1,0:T(1,128)} %get-tuple-element.10) | copy-start | bytes 27652
  103.7 21.5 %copy-start.9 = (f32[1024]{0:T(1024)S(1)}, f32[1024]{0:T(1024)}, u32[]{:S(2)}) copy-start(f32[1024]{0:T(1024)} %param.12) | copy-start | bytes 12292
  106.0 19.2 %collective-permute-start.7 = (bf16[512,512]{1,0:T(8,128)(2,1)}, bf16[512,512]{1,0:T(8,128)(2,1)}, u32[]{:S(2)}, u32[]{:S(2)}) collective-permute-start(bf16[512,512]{1,0:T(8,128)(2,1)} %get-tuple-element.15), channel_id=1, source_target_pairs={{0,4},{4,0},{8,12},{12,8},{16,20},{20,16},{24,28},{28,24},{1,5},{5... | collective-permute-start | bytes 1572872 | tf_op jit(solution)/shard_map/ppermute | solution.py:135
  110.8 13.7 %all-to-all-start.1 = ((f32[32,1,64]{2,1,0:T(1,128)}), f32[32,1,64]{2,1,0:T(1,128)S(1)}, u32[]{:S(2)}, u32[]{:S(2)}) async-start(f32[32,1,64]{2,1,0:T(1,128)} %bitcast.8), calls=%async_computation.1 | async-start | bytes 32768 | tf_op jit(solution)/shard_map/all_to_all | solution.py:127
  119.7 14.4 %collective-permute-start.6 = (bf16[512,512]{1,0:T(8,128)(2,1)}, bf16[512,512]{1,0:T(8,128)(2,1)}, u32[]{:S(2)}, u32[]{:S(2)}) collective-permute-start(bf16[512,512]{1,0:T(8,128)(2,1)} %get-tuple-element.17), channel_id=1, source_target_pairs={{0,4},{4,0},{8,12},{12,8},{16,20},{20,16},{24,28},{28,24},{1,5},{5... | collective-permute-start | bytes 1572872 | tf_op jit(solution)/shard_map/ppermute | solution.py:135
  125.1 9.0 %copy-start.2 = (bf16[512,1024]{1,0:T(8,128)(2,1)S(1)}, bf16[512,1024]{1,0:T(8,128)(2,1)}, u32[]{:S(2)}) copy-start(bf16[512,1024]{1,0:T(8,128)(2,1)} %param.10) | copy-start | bytes 3145732
  125.1 9.0 %copy-start.3 = (bf16[512,1024]{1,0:T(8,128)(2,1)S(1)}, bf16[512,1024]{1,0:T(8,128)(2,1)}, u32[]{:S(2)}) copy-start(bf16[512,1024]{1,0:T(8,128)(2,1)} %param.7) | copy-start | bytes 3145732
  125.1 9.0 %copy-start.7 = (bf16[512,512]{1,0:T(8,128)(2,1)S(1)}, bf16[512,512]{1,0:T(8,128)(2,1)}, u32[]{:S(2)}) copy-start(bf16[512,512]{1,0:T(8,128)(2,1)} %get-tuple-element.18) | copy-start | bytes 1572868
where the time goes:
time: 138 us
  waiting for transfers between devices  60.9 us (44%)
  starting transfers between devices  29.5 us (21%)
  other arithmetic  23.2 us (17%)
  Pallas kernels  14 us (10%)
  local copies, waits for them, and re-layouts  9.36 us (7%)
    ppermute x4, waiting for transfers between devices, shift_pairs(): return lax.ppermute(value, 'ctx', pairs)  19.4 us
    all_to_all x1, waiting for transfers between devices, shards(): lax.all_to_all(grouped.reshape(count * tps, own_taps), ('ctx', 'tp'), 0,...  14.1 us
    pallas_call x1, Pallas kernels, shards(): pl.pallas_call(conv_kernel, out_shape=(jax.ShapeDtypeStruct((big, half),...  14 us
    ppermute x4, starting transfers between devices, shift_pairs(): return lax.ppermute(value, 'ctx', pairs)  12.8 us
    ppermute x1, waiting for transfers between devices, shards(): g0 = join(gk, lax.ppermute(gg, 'ctx', swap))  12.2 us
    ppermute x1, waiting for transfers between devices, shards(): m0 = join(mk, lax.ppermute(mg, 'ctx', swap))  7.68 us
    all_to_all x1, starting transfers between devices, shards(): pieces = lax.all_to_all(lag_sums, ('ctx', 'tp'), 0, 0, tiled=True)  6.6 us
    select_n x2, other arithmetic, restore(): give = jnp.where(low, a[rows:], a[:rows])  4.53 us
  transfers between devices with their start and end apart: 10, of which 7 were waited for; matrix products, arithmetic and copies ran while one was open for 14% of the time, Pallas kernels for 0%

commit v1 on v0

v1 whole, which is shorter than its diff:
```python
import functools
import math

import jax
import jax.numpy as jnp
from jax import lax
from jax.experimental import pallas as pl
from jax.experimental.pallas import tpu as pltpu
from jax.sharding import PartitionSpec as P

FGROUP = 512
FLEN = 2048
C = 256
BAND = FLEN + C
CHUNKS = 2
MESH = pl.DeviceIdType.MESH


def left_diagonals(product):
    total = product[0:8]
    for q in range(1, C // 8):
        total = total + pltpu.roll(product[8 * q : 8 * q + 8], BAND - 8 * q, 1)
    row = lax.broadcasted_iota(jnp.int32, (8, BAND), 0)
    for bit in (1, 2, 4):
        total = jnp.where((row & bit) != 0, pltpu.roll(total, BAND - bit, 1), total)
    return jnp.sum(total, axis=0, keepdims=True)


def pair_kernel(
    half, taps, ids_col, ids_src, ids_grd, query, key, value, ograd,
    conv_out, back_out, diag_out,
    src, grd, give_m, give_g, conv_s, back_s, got_c, got_b,
    taps_all, row_f, row_b, wide, wf, wb, acc, diag_send,
    t_send, t_recv, x_send, x_recv, z_send, z_recv, o_send, o_recv, d_send, d_recv,
):
    count = lax.axis_size("ctx")
    me = lax.axis_index("ctx")
    x = lax.rem(me, 2)
    p = me // 2
    last = count // 2 - 1
    partner = me + 1 - 2 * x
    up = lax.rem(me + 2, count)
    down = lax.rem(me + count - 2, count)
    rows = query.shape[0]
    big = 2 * rows
    chunks, _, cw = src.shape
    tw = taps.shape[1]
    f32 = jnp.float32

    barrier = pltpu.get_barrier_semaphore()
    for d in range(1, count):
        pl.semaphore_signal(barrier, inc=1, device_id={"ctx": lax.rem(me + d, count)}, device_id_type=MESH)
    pl.semaphore_wait(barrier, count - 1)

    def remote(source, target, send, recv, device):
        return pltpu.make_async_remote_copy(
            src_ref=source, dst_ref=target, send_sem=send, recv_sem=recv, device_id={"ctx": device}, device_id_type=MESH
        )

    def at(base, mine):
        offset = x * rows if mine else (1 - x) * rows
        return pl.ds(pl.multiple_of(base + offset, C), rows)

    def columns(own, c):
        offset = x * half if own else (1 - x) * half
        return pl.ds(pl.multiple_of(offset + c * cw, 128), cw)

    tap_copies = [
        remote(taps, taps_all.at[d], t_send.at[d - 1], t_recv.at[d - 1], lax.rem(me + d, count)) for d in range(1, count)
    ]

    def swap_copies(c):
        here = at(0, True)
        return (
            remote(give_m.at[c], src.at[c, at(2 * big, True)], x_send.at[c, 0], x_recv.at[c, 0], partner),
            remote(give_g.at[c], grd.at[c, here], x_send.at[c, 1], x_recv.at[c, 1], partner),
        )

    def hop(c, part, stage):
        mine = part == 0
        index = (c * 2 + part) * 2 + stage
        rising = remote(
            src.at[c, at((2 - stage) * big, mine)], src.at[c, at((1 - stage) * big, mine)],
            z_send.at[0, index], z_recv.at[0, index], up,
        )
        falling = remote(
            grd.at[c, at(stage * big, mine)], grd.at[c, at((1 + stage) * big, mine)],
            z_send.at[1, index], z_recv.at[1, index], down,
        )
        return rising, falling

    def can_send(stage):
        return (p < last) & (p >= stage), (p > 0) & (p <= last - stage)

    def can_receive(stage):
        return p >= 1 + stage, p <= last - 1 - stage

    def start_hop(c, part, stage):
        for copy, ok in zip(hop(c, part, stage), can_send(stage)):
            pl.when(ok)(copy.start)

    def end_hop(c, part, stage):
        for copy, ok in zip(hop(c, part, stage), can_receive(stage)):
            pl.when(ok)(copy.wait_recv)

    for copy in tap_copies:
        copy.start()
    for c in range(chunks):
        cols = columns(False, c)
        give_m[c] = (key[:, cols].astype(f32) * value[:, cols].astype(f32)).astype(jnp.bfloat16)
        swap_copies(c)[0].start()
        give_g[c] = (ograd[:, cols].astype(f32) * query[:, cols].astype(f32)).astype(jnp.bfloat16)
        swap_copies(c)[1].start()
        cols = columns(True, c)
        src[c, at(2 * big, True), :] = (key[:, cols].astype(f32) * value[:, cols].astype(f32)).astype(jnp.bfloat16)
        grd[c, at(0, True), :] = (ograd[:, cols].astype(f32) * query[:, cols].astype(f32)).astype(jnp.bfloat16)
        start_hop(c, 0, 0)

    for stage in range(2):
        low, high = can_receive(stage)

        def blank_src(stage=stage):
            for c in range(chunks):
                src[c, (1 - stage) * big : (2 - stage) * big, :] = jnp.zeros((big, cw), jnp.bfloat16)

        def blank_grd(stage=stage):
            for c in range(chunks):
                grd[c, (1 + stage) * big : (2 + stage) * big, :] = jnp.zeros((big, cw), jnp.bfloat16)

        pl.when(jnp.logical_not(low))(blank_src)
        pl.when(jnp.logical_not(high))(blank_grd)

    taps_all[0] = taps[...]
    for copy in tap_copies:
        copy.wait_recv()
    row_f[...] = jnp.zeros_like(row_f)
    row_b[...] = jnp.zeros_like(row_b)
    own_group = (x * half) // FGROUP
    for j in range(count):
        block = taps_all[lax.rem(me + count - j, count)]
        row_b[:, j * tw : (j + 1) * tw] = jnp.where(own_group == 0, block[0:1], block[1:2])
        m = count - 1 - j
        row_f[:, m * tw : (m + 1) * tw] = jnp.where(own_group == 0, block[2:3], block[3:4])

    def masked(first, shift, ids_row, out):
        wide[...] = pltpu.roll(jnp.broadcast_to(first[...], (C, BAND)), shift, 1, stride=1, stride_axis=0)

        def one(i, carry):
            row = pl.multiple_of(i * C, C)
            mask = ids_col[pl.ds(row, C), :] == ids_row[:, pl.ds(row, BAND)]
            out[i] = jnp.where(mask, wide[...], 0.0).astype(jnp.bfloat16)
            return carry

        lax.fori_loop(0, big // C, one, 0)

    masked(row_f, 1, ids_src, wf)
    end_hop(0, 0, 0)
    start_hop(0, 0, 1)
    masked(row_b, 0, ids_grd, wb)
    acc[...] = jnp.zeros_like(acc)

    def swapped(c):
        for copy in swap_copies(c):
            copy.wait_recv()
        start_hop(c, 1, 0)

    def compute(c):
        def one(i, carry):
            row = pl.multiple_of(i * C, C)
            own, span = pl.ds(row, C), pl.ds(row, BAND)
            source = src[c, span, :]
            conv_s[c, own, :] = jnp.dot(wf[i], source, preferred_element_type=f32).astype(jnp.bfloat16)
            prod = lax.dot_general(grd[c, own, :], source, (((1,), (1,)), ((), ())), preferred_element_type=f32)
            acc[...] += jnp.where(ids_col[own, :] == ids_src[:, span], prod, 0.0)
            back_s[c, own, :] = jnp.dot(wb[i], grd[c, span, :], preferred_element_type=f32).astype(jnp.bfloat16)
            return carry

        lax.fori_loop(0, big // C, one, 0)

    def out_copies(c):
        theirs = at(0, False)
        return (
            remote(conv_s.at[c, theirs], got_c.at[c], o_send.at[c, 0], o_recv.at[c, 0], partner),
            remote(back_s.at[c, theirs], got_b.at[c], o_send.at[c, 1], o_recv.at[c, 1], partner),
        )

    def finish(c):
        cols = columns(True, c)
        conv_out[:, cols] = conv_s[c, at(0, True), :]
        back_out[:, cols] = back_s[c, at(0, True), :]
        for copy in out_copies(c):
            copy.wait_recv()
        cols = columns(False, c)
        conv_out[:, cols] = got_c[c]
        back_out[:, cols] = got_b[c]

    swapped(0)
    end_hop(0, 1, 0)
    start_hop(0, 1, 1)
    for c in range(chunks):
        if c + 1 < chunks:
            end_hop(c + 1, 0, 0)
            start_hop(c + 1, 0, 1)
            swapped(c + 1)
        end_hop(c, 0, 1)
        end_hop(c, 1, 1)
        compute(c)
        for copy in out_copies(c):
            copy.start()
        if c + 1 < chunks:
            end_hop(c + 1, 1, 0)
            start_hop(c + 1, 1, 1)

    sums = pltpu.roll(left_diagonals(acc[...]), BAND - 1, 1)
    wide[0:1, :] = sums
    for j in range(count):
        m = count - 1 - j
        diag_send[j] = jnp.broadcast_to(wide[0:1, m * tw : (m + 1) * tw], (8, tw))
    diag_copies = []
    for d in range(1, count):
        peer = lax.rem(me + d, count)
        diag_copies.append(remote(diag_send.at[peer], diag_out.at[d], d_send.at[d - 1], d_recv.at[d - 1], peer))
    for copy in diag_copies:
        copy.start()
    diag_out[0] = diag_send[me]
    for c in range(chunks):
        finish(c)
    for copy in diag_copies:
        copy.wait_recv()
    for copy in tap_copies + diag_copies:
        copy.wait_send()
    for c in range(chunks):
        for copy in swap_copies(c) + out_copies(c):
            copy.wait_send()
        for part in range(2):
            for stage in range(2):
                for copy, ok in zip(hop(c, part, stage), can_send(stage)):
                    pl.when(ok)(copy.wait_send)


def shards(query_in, key_in, value_in, out_grad, doc_ids, skip_gain, filter_taps):
    rows, width = query_in.shape
    half = width // 2
    chunks = CHUNKS
    cw = half // chunks
    count = lax.axis_size("ctx")
    here = lax.axis_index("ctx")
    pair = here // 2
    big = 2 * rows
    bf16, f32 = jnp.bfloat16, jnp.float32

    local = lax.all_to_all(filter_taps, "tp", split_axis=1, concat_axis=0, tiled=True).T.astype(f32)
    held, tw = local.shape
    both = jnp.broadcast_to(local[:, None], (held, 2 // held, tw)).reshape(2, tw)
    taps = jnp.concatenate([both, both[:, ::-1], jnp.zeros((4, tw), f32)], axis=0)

    none = jnp.full((2 * big,), -1, jnp.int32)
    ids = jnp.concatenate([none, doc_ids, none])
    near = lax.dynamic_slice_in_dim(ids, pair * big, 5 * big)
    ids_src = near[: 3 * big].reshape(1, -1)
    ids_grd = near[2 * big :].reshape(1, -1)
    ids_col = near[2 * big : 3 * big].reshape(-1, 1)

    dma = pltpu.SemaphoreType.DMA
    conv, back, diag = pl.pallas_call(
        functools.partial(pair_kernel, half),
        out_shape=(
            jax.ShapeDtypeStruct((rows, width), bf16),
            jax.ShapeDtypeStruct((rows, width), bf16),
            jax.ShapeDtypeStruct((count, 8, tw), f32),
        ),
        in_specs=[pl.BlockSpec(memory_space=pltpu.VMEM)] * 8,
        out_specs=(pl.BlockSpec(memory_space=pltpu.VMEM),) * 3,
        scratch_shapes=[
            pltpu.VMEM((chunks, 3 * big, cw), bf16),
            pltpu.VMEM((chunks, 3 * big, cw), bf16),
            pltpu.VMEM((chunks, rows, cw), bf16),
            pltpu.VMEM((chunks, rows, cw), bf16),
            pltpu.VMEM((chunks, big, cw), bf16),
            pltpu.VMEM((chunks, big, cw), bf16),
            pltpu.VMEM((chunks, rows, cw), bf16),
            pltpu.VMEM((chunks, rows, cw), bf16),
            pltpu.VMEM((count, 8, tw), f32),
            pltpu.VMEM((1, BAND), f32),
            pltpu.VMEM((1, BAND), f32),
            pltpu.VMEM((C, BAND), f32),
            pltpu.VMEM((big // C, C, BAND), bf16),
            pltpu.VMEM((big // C, C, BAND), bf16),
            pltpu.VMEM((C, BAND), f32),
            pltpu.VMEM((count, 8, tw), f32),
            dma((count - 1,)), dma((count - 1,)),
            dma((chunks, 2)), dma((chunks, 2)),
            dma((2, 4 * chunks)), dma((2, 4 * chunks)),
            dma((chunks, 2)), dma((chunks, 2)),
            dma((count - 1,)), dma((count - 1,)),
        ],
        compiler_params=pltpu.CompilerParams(
            collective_id=0, has_side_effects=True, vmem_limit_bytes=58 * 1024 * 1024
        ),
    )(taps, ids_col, ids_src, ids_grd, query_in, key_in, value_in, out_grad)

    sender = lax.rem(here + count - jnp.arange(count), count)
    odd = (sender % 2 == 1)[:, None]
    each = diag[:, 0, ::-1]
    scale = 1.0 / math.sqrt(FGROUP * count * rows)
    parts = jnp.stack([jnp.where(odd, 0.0, each).sum(0), jnp.where(odd, each, 0.0).sum(0)])
    scaled = parts.reshape(held, 2 // held, tw).sum(1).T * scale
    filter_grad = lax.all_to_all(scaled, "tp", split_axis=0, concat_axis=1, tiled=True)

    skip = skip_gain[None, :]
    key_f, value_f = key_in.astype(f32), value_in.astype(f32)
    query_f, grad_f = query_in.astype(f32), out_grad.astype(f32)
    conv = skip * (key_f * value_f).astype(bf16).astype(f32) + conv.astype(f32)
    mgrad = skip * (grad_f * query_f).astype(bf16).astype(f32) + back.astype(f32)
    return (
        (query_f * conv).astype(bf16),
        (grad_f * conv).astype(bf16),
        (mgrad * value_f).astype(bf16),
        (mgrad * key_f).astype(bf16),
        filter_grad,
    )


def solution(mesh):
    in_specs = (
        P("ctx", "tp"),
        P("ctx", "tp"),
        P("ctx", "tp"),
        P("ctx", "tp"),
        P(),
        P("tp"),
        P(("ctx", "tp"), None),
    )
    out_specs = (
        P("ctx", "tp"),
        P("ctx", "tp"),
        P("ctx", "tp"),
        P("ctx", "tp"),
        P(("ctx", "tp"), None),
    )
    return jax.shard_map(shards, mesh=mesh, in_specs=in_specs, out_specs=out_specs, check_vma=False)
```

time: 138 us -> 96.5 us (0.70)
  waiting for transfers between devices: 60.9 us -> 1.21 us
  Pallas kernels: 14 us -> 73.4 us
  starting transfers between devices: 29.5 us -> 7.81 us
  other arithmetic: 23.2 us -> 8.07 us
  local copies, waits for them, and re-layouts: 9.36 us -> 5.02 us
    pallas_call x1, Pallas kernels: 14 us -> 73.4 us  [shards(): pl.pallas_call(functools.partial(pair_kernel, half), out_shape=(jax.Shape...]
    ppermute x8 -> x0, waiting for transfers between devices: 43.7 us -> none  [the longest x4 19.4 us: shift_pairs(): return lax.ppermute(value, 'ctx', pairs)]
    ppermute x8 -> x0, starting transfers between devices: 19.2 us -> none  [the longest x4 12.8 us: shift_pairs(): return lax.ppermute(value, 'ctx', pairs)]
    all_to_all x2, waiting for transfers between devices: 17.2 us -> 1.21 us  [the longest x1 1.21 us: shards(): lax.all_to_all(filter_taps, 'tp', split_axis=1, concat_axis=0, tiled=True)]
    select_n x6 -> x0, other arithmetic: 5.6 us -> none  [the longest x2 4.53 us: restore(): give = jnp.where(low, a[rows:], a[:rows])]
    concatenate x2 -> x1, other arithmetic: 6.19 us -> 0.67 us  [shards(): jnp.concatenate([both, both[:, ::-1], jnp.zeros((4, tw), f32)], axis=0)]
    convert_element_type x5 -> x2, other arithmetic: 10.6 us -> 5.9 us  [the longest x1 5.9 us: shards(): (mgrad * key_f).astype(bf16)]
    rev x3 -> x2, local copies, waits for them, and re-layouts: 3.33 us -> 0.41 us  [the longest x1 0.23 us: shards(): each = diag[:, 0, ::-1]]
  transfers between devices with their start and end apart: 10 -> 2, of which waited for: 7 -> 1; matrix products, arithmetic and copies ran while one was open for 14% -> 9% of each run, Pallas kernels for 0% -> 0%
where the time goes in v1:
time: 96.5 us; the launch traced here: 96.2 us
  Pallas kernels  73.4 us (76%)
  other arithmetic  8.07 us (8%)
  starting transfers between devices  7.81 us (8%)
  local copies, waits for them, and re-layouts  5.02 us (5%)
  waiting for transfers between devices  1.21 us (1%)
    pallas_call x1, Pallas kernels, shards(): pl.pallas_call(functools.partial(pair_kernel, half), out_shape=(jax.Shape...  73.4 us
    convert_element_type x1, other arithmetic, shards(): (mgrad * key_f).astype(bf16)  5.9 us
    all_to_all x1, starting transfers between devices, shards(): lax.all_to_all(filter_taps, 'tp', split_axis=1, concat_axis=0, tiled=True)  4.25 us
    all_to_all x1, starting transfers between devices, shards(): lax.all_to_all(scaled, 'tp', split_axis=0, concat_axis=1, tiled=True)  3.57 us
  transfers between devices with their start and end apart: 2, of which 1 were waited for; matrix products, arithmetic and copies ran while one was open for 9% of the time, Pallas kernels for 0%

profile of v1, /device:TPU:0, one launch (start us, length us, event | category | flops | bytes accessed | tf_op | source)
XLA Modules:
  0.0 96.2 jit_solution(9457930221726935399)
XLA Ops:
  0.6 4.2 %all-to-all-start = ((bf16[64,4,2]{0,2,1:T(2,128)(2,1)}), bf16[64,4,2]{0,2,1:T(2,128)(2,1)S(1)}, u32[]{:S(2)}, u32[]{:S(2)}) async-start(bf16[64,4,2]{0,2,1:T(2,128)(2,1)} %bitcast.38), calls=%async_computation | async-start | bytes 4096 | tf_op jit(solution)/shard_map/all_to_all | solution.py:252
  4.9 0.7 fusion.7
  5.6 0.6 fusion.14
  6.2 1.0 %copy.19.ids_col = s32[1024,1]{1,0:T(8,128)} copy(s32[1024,1]{0,1:T(1,128)S(1)} %bitcast.33) | data formatting | bytes 8192 | tf_op jit(solution)/shard_map/reshape | solution.py:262
  7.3 0.1 pad.7.clone
  7.3 1.2 %all-to-all-done = bf16[64,4,2]{0,2,1:T(2,128)(2,1)S(1)} async-done(((bf16[64,4,2]{0,2,1:T(2,128)(2,1)}), bf16[64,4,2]{0,2,1:T(2,128)(2,1)S(1)}, u32[]{:S(2)}, u32[]{:S(2)}) %all-to-all-start) | async-done | bytes 1056 | tf_op jit(solution)/shard_map/all_to_all | solution.py:252
  8.6 0.1 reshape.56
  8.7 0.2 rev.6
  8.8 0.7 maximum_maximum_fusion.taps
  9.5 73.4 %shard_map.110 = (bf16[512,1024]{1,0:T(8,128)(2,1)}, bf16[512,1024]{1,0:T(8,128)(2,1)}, f32[8,8,256]{2,1,0:T(8,128)}) custom-call(f32[8,256]{1,0:T(8,128)} %maximum_maximum_fusion.taps, s32[1024,1]{1,0:T(8,128)} %copy.19.ids_col, s32[1,3072]{1,0:T(1,128)} %bitcast.30, s32[1,3072]{1,0:T(1,128)} %bitcast.29, bf16[512,1024]{1,0:T(8,128)(2,1)} %query.1, ...), custom_call_target="tpu_custom_call" | custom-call | tf_op jit(solution)/shard_map/pallas_call | solution.py:265
  82.9 0.8 slice.15
  83.7 0.2 rev.7
  84.0 0.1 fusion.8
  84.1 0.1 all_to_all.26
  84.2 0.7 reshape.57
  84.8 3.6 %all-to-all-start.1 = ((f32[4,1,128]{2,1,0:T(1,128)}), f32[4,1,128]{2,1,0:T(1,128)S(1)}, u32[]{:S(2)}, u32[]{:S(2)}) async-start(f32[4,1,128]{2,1,0:T(1,128)} %reshape.57), calls=%async_computation.1 | async-start | bytes 4096 | tf_op jit(solution)/shard_map/all_to_all | solution.py:308
  88.4 0.0 copy-done
  88.4 0.0 copy-done.1
  88.4 0.0 copy-done.3
  88.4 5.9 %fusion.1 = (bf16[512,1024]{1,0:T(8,128)(2,1)}, bf16[512,1024]{1,0:T(8,128)(2,1)}, bf16[512,1024]{1,0:T(8,128)(2,1)}, bf16[512,1024]{1,0:T(8,128)(2,1)}) fusion(bf16[512,1024]{1,0:T(8,128)(2,1)S(1)} %copy-done, bf16[512,1024]{1,0:T(8,128)(2,1)} %get-tuple-element.9, f32[1024]{0:T(1024)S(1)} %copy-done.3, bf16[512,1024]{1,0:T(8,128)(2,1)S(1)} %copy-done.1, ...), kind=kLoop, calls=%fused_computation.7 | loop fusion | flops 12582912 | bytes 10489856 | tf_op jit(solution)/shard_map/convert_element_type | solution.py:319
  94.3 0.0 all-to-all-done.1
  94.3 0.5 broadcast.53
  94.8 0.7 reduce
  95.5 0.7 reshape.58
  (13 shorter events, 0.1 us)
Async XLA Ops:
  0.6 7.9 %all-to-all-start = ((bf16[64,4,2]{0,2,1:T(2,128)(2,1)}), bf16[64,4,2]{0,2,1:T(2,128)(2,1)S(1)}, u32[]{:S(2)}, u32[]{:S(2)}) async-start(bf16[64,4,2]{0,2,1:T(2,128)(2,1)} %bitcast.38), calls=%async_computation | async-start | bytes 4096 | tf_op jit(solution)/shard_map/all_to_all | solution.py:252
  9.5 78.9 %copy-start = (bf16[512,1024]{1,0:T(8,128)(2,1)S(1)}, bf16[512,1024]{1,0:T(8,128)(2,1)}, u32[]{:S(2)}) copy-start(bf16[512,1024]{1,0:T(8,128)(2,1)} %key.1) | copy-start | bytes 3145732
  9.5 78.9 %copy-start.1 = (bf16[512,1024]{1,0:T(8,128)(2,1)S(1)}, bf16[512,1024]{1,0:T(8,128)(2,1)}, u32[]{:S(2)}) copy-start(bf16[512,1024]{1,0:T(8,128)(2,1)} %query.1) | copy-start | bytes 3145732
  9.5 78.9 %copy-start.2 = (bf16[512,1024]{1,0:T(8,128)(2,1)S(1)}, bf16[512,1024]{1,0:T(8,128)(2,1)}, u32[]{:S(2)}) copy-start(bf16[512,1024]{1,0:T(8,128)(2,1)} %value.1) | copy-start | bytes 3145732
  9.5 78.9 %copy-start.3 = (f32[1024]{0:T(1024)S(1)}, f32[1024]{0:T(1024)}, u32[]{:S(2)}) copy-start(f32[1024]{0:T(1024)} %param.12) | copy-start | bytes 12292
  84.8 9.5 %all-to-all-start.1 = ((f32[4,1,128]{2,1,0:T(1,128)}), f32[4,1,128]{2,1,0:T(1,128)S(1)}, u32[]{:S(2)}, u32[]{:S(2)}) async-start(f32[4,1,128]{2,1,0:T(1,128)} %reshape.57), calls=%async_computation.1 | async-start | bytes 4096 | tf_op jit(solution)/shard_map/all_to_all | solution.py:308

commit v2 on v1

--- a/solution.py
+++ b/solution.py
@@ -12,7 +12,7 @@
 FLEN = 2048
 C = 256
 BAND = FLEN + C
-CHUNKS = 2
+CHUNKS = 4
 MESH = pl.DeviceIdType.MESH
 
 
@@ -105,7 +105,9 @@
 
     for copy in tap_copies:
         copy.start()
-    for c in range(chunks):
+    def begin(c):
+        if c >= chunks:
+            return
         cols = columns(False, c)
         give_m[c] = (key[:, cols].astype(f32) * value[:, cols].astype(f32)).astype(jnp.bfloat16)
         swap_copies(c)[0].start()
@@ -115,6 +117,9 @@
         src[c, at(2 * big, True), :] = (key[:, cols].astype(f32) * value[:, cols].astype(f32)).astype(jnp.bfloat16)
         grd[c, at(0, True), :] = (ograd[:, cols].astype(f32) * query[:, cols].astype(f32)).astype(jnp.bfloat16)
         start_hop(c, 0, 0)
+
+    begin(0)
+    begin(1)
 
     for stage in range(2):
         low, high = can_receive(stage)
@@ -163,8 +168,9 @@
         for copy in swap_copies(c):
             copy.wait_recv()
         start_hop(c, 1, 0)
-
-    def compute(c):
+        begin(c + 2)
+
+    def compute(c, first, end):
         def one(i, carry):
             row = pl.multiple_of(i * C, C)
             own, span = pl.ds(row, C), pl.ds(row, BAND)
@@ -175,7 +181,7 @@
             back_s[c, own, :] = jnp.dot(wb[i], grd[c, span, :], preferred_element_type=f32).astype(jnp.bfloat16)
             return carry
 
-        lax.fori_loop(0, big // C, one, 0)
+        lax.fori_loop(first, end, one, 0)
 
     def out_copies(c):
         theirs = at(0, False)
@@ -194,22 +200,30 @@
         conv_out[:, cols] = got_c[c]
         back_out[:, cols] = got_b[c]
 
+    def forward_first(c):
+        if c < chunks:
+            end_hop(c, 0, 0)
+            start_hop(c, 0, 1)
+            swapped(c)
+
+    def forward_second(c):
+        if c < chunks:
+            end_hop(c, 1, 0)
+            start_hop(c, 1, 1)
+
     swapped(0)
-    end_hop(0, 1, 0)
-    start_hop(0, 1, 1)
+    forward_second(0)
+    forward_first(1)
+    middle = big // C // 2
     for c in range(chunks):
-        if c + 1 < chunks:
-            end_hop(c + 1, 0, 0)
-            start_hop(c + 1, 0, 1)
-            swapped(c + 1)
+        forward_first(c + 2)
         end_hop(c, 0, 1)
         end_hop(c, 1, 1)
-        compute(c)
+        compute(c, 0, middle)
+        forward_second(c + 1)
+        compute(c, middle, big // C)
         for copy in out_copies(c):
             copy.start()
-        if c + 1 < chunks:
-            end_hop(c + 1, 1, 0)
-            start_hop(c + 1, 1, 1)
 
     sums = pltpu.roll(left_diagonals(acc[...]), BAND - 1, 1)
     wide[0:1, :] = sums
@@ -241,7 +255,7 @@
 def shards(query_in, key_in, value_in, out_grad, doc_ids, skip_gain, filter_taps):
     rows, width = query_in.shape
     half = width // 2
-    chunks = CHUNKS
+    chunks = max(1, min(CHUNKS, half // 128))
     cw = half // chunks
     count = lax.axis_size("ctx")
     here = lax.axis_index("ctx")
@@ -310,8 +324,8 @@
     skip = skip_gain[None, :]
     key_f, value_f = key_in.astype(f32), value_in.astype(f32)
     query_f, grad_f = query_in.astype(f32), out_grad.astype(f32)
-    conv = skip * (key_f * value_f).astype(bf16).astype(f32) + conv.astype(f32)
-    mgrad = skip * (grad_f * query_f).astype(bf16).astype(f32) + back.astype(f32)
+    conv = skip * lax.reduce_precision(key_f * value_f, 8, 7) + conv.astype(f32)
+    mgrad = skip * lax.reduce_precision(grad_f * query_f, 8, 7) + back.astype(f32)
     return (
         (query_f * conv).astype(bf16),
         (grad_f * conv).astype(bf16),

time: 96.5 us -> 93.6 us (0.970)
  Pallas kernels: 73.4 us -> 70.5 us
    pallas_call x1, Pallas kernels: 73.4 us -> 70.5 us  [shards(): pl.pallas_call(functools.partial(pair_kernel, half), out_shape=(jax.Shape...]
where the time goes in v2:
time: 93.6 us; the launch traced here: 93.2 us
  Pallas kernels  70.5 us (75%)
  other arithmetic  8.16 us (9%)
  starting transfers between devices  7.65 us (8%)
  local copies, waits for them, and re-layouts  5.02 us (5%)
  waiting for transfers between devices  1.21 us (1%)
    pallas_call x1, Pallas kernels, shards(): pl.pallas_call(functools.partial(pair_kernel, half), out_shape=(jax.Shape...  70.5 us
    convert_element_type x1, other arithmetic, shards(): (mgrad * key_f).astype(bf16)  5.99 us
    all_to_all x1, starting transfers between devices, shards(): lax.all_to_all(filter_taps, 'tp', split_axis=1, concat_axis=0, tiled=True)  4.25 us
    all_to_all x1, starting transfers between devices, shards(): lax.all_to_all(scaled, 'tp', split_axis=0, concat_axis=1, tiled=True)  3.4 us
  transfers between devices with their start and end apart: 2, of which 1 were waited for; matrix products, arithmetic and copies ran while one was open for 9% of the time, Pallas kernels for 0%

profile of v2, /device:TPU:0, one launch (start us, length us, event | category | flops | bytes accessed | tf_op | source)
XLA Modules:
  0.0 93.2 jit_solution(11143270295684665129)
XLA Ops:
  0.6 4.2 %all-to-all-start = ((bf16[64,4,2]{0,2,1:T(2,128)(2,1)}), bf16[64,4,2]{0,2,1:T(2,128)(2,1)S(1)}, u32[]{:S(2)}, u32[]{:S(2)}) async-start(bf16[64,4,2]{0,2,1:T(2,128)(2,1)} %bitcast.38), calls=%async_computation | async-start | bytes 4096 | tf_op jit(solution)/shard_map/all_to_all | solution.py:266
  4.9 0.7 fusion.11
  5.6 0.6 fusion.18
  6.2 1.0 %copy.19.ids_col = s32[1024,1]{1,0:T(8,128)} copy(s32[1024,1]{0,1:T(1,128)S(1)} %bitcast.33) | data formatting | bytes 8192 | tf_op jit(solution)/shard_map/reshape | solution.py:276
  7.3 0.1 pad.7.clone
  7.3 1.2 %all-to-all-done = bf16[64,4,2]{0,2,1:T(2,128)(2,1)S(1)} async-done(((bf16[64,4,2]{0,2,1:T(2,128)(2,1)}), bf16[64,4,2]{0,2,1:T(2,128)(2,1)S(1)}, u32[]{:S(2)}, u32[]{:S(2)}) %all-to-all-start) | async-done | bytes 1056 | tf_op jit(solution)/shard_map/all_to_all | solution.py:266
  8.6 0.1 reshape.56
  8.7 0.2 rev.6
  8.8 0.7 maximum_maximum_fusion.taps
  9.5 70.5 %shard_map.110 = (bf16[512,1024]{1,0:T(8,128)(2,1)}, bf16[512,1024]{1,0:T(8,128)(2,1)}, f32[8,8,256]{2,1,0:T(8,128)}) custom-call(f32[8,256]{1,0:T(8,128)} %maximum_maximum_fusion.taps, s32[1024,1]{1,0:T(8,128)} %copy.19.ids_col, s32[1,3072]{1,0:T(1,128)} %bitcast.30, s32[1,3072]{1,0:T(1,128)} %bitcast.29, bf16[512,1024]{1,0:T(8,128)(2,1)} %query.1, ...), custom_call_target="tpu_custom_call" | custom-call | tf_op jit(solution)/shard_map/pallas_call | solution.py:279
  80.0 0.8 slice.15
  80.9 0.2 rev.7
  81.1 0.1 fusion.12
  81.2 0.1 all_to_all.26
  81.3 0.7 reshape.57
  81.9 3.4 %all-to-all-start.1 = ((f32[4,1,128]{2,1,0:T(1,128)}), f32[4,1,128]{2,1,0:T(1,128)S(1)}, u32[]{:S(2)}, u32[]{:S(2)}) async-start(f32[4,1,128]{2,1,0:T(1,128)} %reshape.57), calls=%async_computation.1 | async-start | bytes 4096 | tf_op jit(solution)/shard_map/all_to_all | solution.py:322
  85.4 0.0 copy-done
  85.4 0.0 copy-done.1
  85.4 0.0 copy-done.2
  85.4 6.0 %fusion.1 = (bf16[512,1024]{1,0:T(8,128)(2,1)}, bf16[512,1024]{1,0:T(8,128)(2,1)}, bf16[512,1024]{1,0:T(8,128)(2,1)}, bf16[512,1024]{1,0:T(8,128)(2,1)}) fusion(bf16[512,1024]{1,0:T(8,128)(2,1)S(1)} %copy-done, bf16[512,1024]{1,0:T(8,128)(2,1)} %get-tuple-element.9, bf16[512,1024]{1,0:T(8,128)(2,1)S(1)} %copy-done.1, bf16[512,1024]{1,0:T(8,128)(2,1)} %ograd.1, ...), kind=kLoop, calls=%fused_computation.7 | loop fusion | flops 11534336 | bytes 10489856 | tf_op jit(solution)/shard_map/convert_element_type | solution.py:333
  91.4 0.0 all-to-all-done.1
  91.4 0.5 broadcast.53
  91.9 0.7 reduce
  92.6 0.7 reshape.58
  (13 shorter events, 0.1 us)
Async XLA Ops:
  0.6 7.9 %all-to-all-start = ((bf16[64,4,2]{0,2,1:T(2,128)(2,1)}), bf16[64,4,2]{0,2,1:T(2,128)(2,1)S(1)}, u32[]{:S(2)}, u32[]{:S(2)}) async-start(bf16[64,4,2]{0,2,1:T(2,128)(2,1)} %bitcast.38), calls=%async_computation | async-start | bytes 4096 | tf_op jit(solution)/shard_map/all_to_all | solution.py:266
  9.5 75.9 %copy-start = (bf16[512,1024]{1,0:T(8,128)(2,1)S(1)}, bf16[512,1024]{1,0:T(8,128)(2,1)}, u32[]{:S(2)}) copy-start(bf16[512,1024]{1,0:T(8,128)(2,1)} %key.1) | copy-start | bytes 3145732
  9.5 75.9 %copy-start.1 = (bf16[512,1024]{1,0:T(8,128)(2,1)S(1)}, bf16[512,1024]{1,0:T(8,128)(2,1)}, u32[]{:S(2)}) copy-start(bf16[512,1024]{1,0:T(8,128)(2,1)} %query.1) | copy-start | bytes 3145732
  9.5 75.9 %copy-start.2 = (bf16[512,1024]{1,0:T(8,128)(2,1)S(1)}, bf16[512,1024]{1,0:T(8,128)(2,1)}, u32[]{:S(2)}) copy-start(bf16[512,1024]{1,0:T(8,128)(2,1)} %value.1) | copy-start | bytes 3145732
  9.5 75.9 %copy-start.3 = (f32[1024]{0:T(1024)S(1)}, f32[1024]{0:T(1024)}, u32[]{:S(2)}) copy-start(f32[1024]{0:T(1024)} %param.12) | copy-start | bytes 12292
  81.9 9.4 %all-to-all-start.1 = ((f32[4,1,128]{2,1,0:T(1,128)}), f32[4,1,128]{2,1,0:T(1,128)S(1)}, u32[]{:S(2)}, u32[]{:S(2)}) async-start(f32[4,1,128]{2,1,0:T(1,128)} %reshape.57), calls=%async_computation.1 | async-start | bytes 4096 | tf_op jit(solution)/shard_map/all_to_all | solution.py:322

commit v3 on v2

--- a/solution.py
+++ b/solution.py
@@ -27,11 +27,11 @@
 
 
 def pair_kernel(
-    half, taps, ids_col, ids_src, ids_grd, query, key, value, ograd,
-    conv_out, back_out, diag_out,
+    half, taps_tp, ids_col, ids_src, ids_grd, query, key, value, ograd,
+    conv_out, back_out, sums_out,
     src, grd, give_m, give_g, conv_s, back_s, got_c, got_b,
-    taps_all, row_f, row_b, wide, wf, wb, acc, diag_send,
-    t_send, t_recv, x_send, x_recv, z_send, z_recv, o_send, o_recv, d_send, d_recv,
+    taps_all, row_f, row_b, wide, wf, wb, acc, diag_send, diag_in, taps, taps_in, sums_send, sums_in,
+    t_send, t_recv, x_send, x_recv, z_send, z_recv, o_send, o_recv, d_send, d_recv, a_send, a_recv, b_send, b_recv,
 ):
     count = lax.axis_size("ctx")
     me = lax.axis_index("ctx")
@@ -50,11 +50,17 @@
     barrier = pltpu.get_barrier_semaphore()
     for d in range(1, count):
         pl.semaphore_signal(barrier, inc=1, device_id={"ctx": lax.rem(me + d, count)}, device_id_type=MESH)
-    pl.semaphore_wait(barrier, count - 1)
-
-    def remote(source, target, send, recv, device):
+    tps = lax.axis_size("tp")
+    lane = lax.axis_index("tp")
+    for d in range(1, tps):
+        pl.semaphore_signal(barrier, inc=1, device_id={"tp": lax.rem(lane + d, tps)}, device_id_type=MESH)
+    pl.semaphore_wait(barrier, count - 1 + tps - 1)
+    own_taps = taps_tp.shape[2]
+    held = sums_out.shape[0] // tps
+
+    def remote(source, target, send, recv, device, axis="ctx"):
         return pltpu.make_async_remote_copy(
-            src_ref=source, dst_ref=target, send_sem=send, recv_sem=recv, device_id={"ctx": device}, device_id_type=MESH
+            src_ref=source, dst_ref=target, send_sem=send, recv_sem=recv, device_id={axis: device}, device_id_type=MESH
         )
 
     def at(base, mine):
@@ -103,7 +109,11 @@
         for copy, ok in zip(hop(c, part, stage), can_receive(stage)):
             pl.when(ok)(copy.wait_recv)
 
-    for copy in tap_copies:
+    first_copies = []
+    for d in range(1, tps):
+        peer = lax.rem(lane + d, tps)
+        first_copies.append(remote(taps_tp.at[peer], taps_in.at[d], a_send.at[d - 1], a_recv.at[d - 1], peer, "tp"))
+    for copy in first_copies:
         copy.start()
     def begin(c):
         if c >= chunks:
@@ -135,7 +145,39 @@
         pl.when(jnp.logical_not(low))(blank_src)
         pl.when(jnp.logical_not(high))(blank_grd)
 
+    taps_in[0] = taps_tp[lane]
+    for copy in first_copies:
+        copy.wait_recv()
+    for t in range(tps):
+        block = taps_in[lax.rem(lane + tps - t, tps)]
+        taps[0:2, t * own_taps : (t + 1) * own_taps] = block[0:2]
+        m = tps - 1 - t
+        taps[2:4, m * own_taps : (m + 1) * own_taps] = block[2:4]
+    taps[4:8, :] = jnp.zeros((4, tw), f32)
+    for copy in tap_copies:
+        copy.start()
     taps_all[0] = taps[...]
+    def swapped(c):
+        for copy in swap_copies(c):
+            copy.wait_recv()
+        start_hop(c, 1, 0)
+        begin(c + 2)
+
+    def forward_first(c):
+        if c < chunks:
+            end_hop(c, 0, 0)
+            start_hop(c, 0, 1)
+            swapped(c)
+
+    def forward_second(c):
+        if c < chunks:
+            end_hop(c, 1, 0)
+            start_hop(c, 1, 1)
+
+    forward_first(0)
+    forward_second(0)
+    forward_first(1)
+
     for copy in tap_copies:
         copy.wait_recv()
     row_f[...] = jnp.zeros_like(row_f)
@@ -159,16 +201,8 @@
         lax.fori_loop(0, big // C, one, 0)
 
     masked(row_f, 1, ids_src, wf)
-    end_hop(0, 0, 0)
-    start_hop(0, 0, 1)
     masked(row_b, 0, ids_grd, wb)
     acc[...] = jnp.zeros_like(acc)
-
-    def swapped(c):
-        for copy in swap_copies(c):
-            copy.wait_recv()
-        start_hop(c, 1, 0)
-        begin(c + 2)
 
     def compute(c, first, end):
         def one(i, carry):
@@ -200,20 +234,6 @@
         conv_out[:, cols] = got_c[c]
         back_out[:, cols] = got_b[c]
 
-    def forward_first(c):
-        if c < chunks:
-            end_hop(c, 0, 0)
-            start_hop(c, 0, 1)
-            swapped(c)
-
-    def forward_second(c):
-        if c < chunks:
-            end_hop(c, 1, 0)
-            start_hop(c, 1, 1)
-
-    swapped(0)
-    forward_second(0)
-    forward_first(1)
     middle = big // C // 2
     for c in range(chunks):
         forward_first(c + 2)
@@ -233,15 +253,42 @@
     diag_copies = []
     for d in range(1, count):
         peer = lax.rem(me + d, count)
-        diag_copies.append(remote(diag_send.at[peer], diag_out.at[d], d_send.at[d - 1], d_recv.at[d - 1], peer))
+        diag_copies.append(remote(diag_send.at[peer], diag_in.at[d], d_send.at[d - 1], d_recv.at[d - 1], peer))
     for copy in diag_copies:
         copy.start()
-    diag_out[0] = diag_send[me]
-    for c in range(chunks):
+    diag_in[0] = diag_send[me]
+    for c in range(chunks - 1):
         finish(c)
     for copy in diag_copies:
         copy.wait_recv()
-    for copy in tap_copies + diag_copies:
+    even = jnp.zeros((1, tw), f32)
+    odd = jnp.zeros((1, tw), f32)
+    for d in range(count):
+        term = diag_in[d, 0:1]
+        flip = lax.rem(me + count - d, 2) == 1
+        even = even + jnp.where(flip, 0.0, term)
+        odd = odd + jnp.where(flip, term, 0.0)
+    if held == 1:
+        even = even + odd
+    wide[0:1, 0:tw] = even
+    wide[1:2, 0:tw] = odd
+    for t in range(tps):
+        m = tps - 1 - t
+        sums_send[t, 0:2, :] = wide[0:2, m * own_taps : (m + 1) * own_taps]
+        sums_send[t, 2:8, :] = jnp.zeros((6, own_taps), f32)
+    last_copies = []
+    for d in range(1, tps):
+        peer = lax.rem(lane + d, tps)
+        last_copies.append(remote(sums_send.at[peer], sums_in.at[d], b_send.at[d - 1], b_recv.at[d - 1], peer, "tp"))
+    for copy in last_copies:
+        copy.start()
+    sums_in[0] = sums_send[lane]
+    finish(chunks - 1)
+    for copy in last_copies:
+        copy.wait_recv()
+    for t in range(tps):
+        sums_out[t * held : (t + 1) * held, :] = sums_in[lax.rem(lane + tps - t, tps), 0:held]
+    for copy in first_copies + tap_copies + diag_copies + last_copies:
         copy.wait_send()
     for c in range(chunks):
         for copy in swap_copies(c) + out_copies(c):
@@ -263,10 +310,13 @@
     big = 2 * rows
     bf16, f32 = jnp.bfloat16, jnp.float32
 
-    local = lax.all_to_all(filter_taps, "tp", split_axis=1, concat_axis=0, tiled=True).T.astype(f32)
-    held, tw = local.shape
-    both = jnp.broadcast_to(local[:, None], (held, 2 // held, tw)).reshape(2, tw)
-    taps = jnp.concatenate([both, both[:, ::-1], jnp.zeros((4, tw), f32)], axis=0)
+    tps = lax.axis_size("tp")
+    own_taps, groups = filter_taps.shape
+    held = groups // tps
+    tw = own_taps * tps
+    grouped = filter_taps.T.astype(f32).reshape(tps, held, 1, own_taps)
+    grouped = jnp.broadcast_to(grouped, (tps, held, 2 // held, own_taps)).reshape(tps, 2, own_taps)
+    taps_tp = jnp.concatenate([grouped, grouped[:, :, ::-1], jnp.zeros((tps, 4, own_taps), f32)], axis=1)
 
     none = jnp.full((2 * big,), -1, jnp.int32)
     ids = jnp.concatenate([none, doc_ids, none])
@@ -276,12 +326,12 @@
     ids_col = near[2 * big : 3 * big].reshape(-1, 1)
 
     dma = pltpu.SemaphoreType.DMA
-    conv, back, diag = pl.pallas_call(
+    conv, back, sums = pl.pallas_call(
         functools.partial(pair_kernel, half),
         out_shape=(
             jax.ShapeDtypeStruct((rows, width), bf16),
             jax.ShapeDtypeStruct((rows, width), bf16),
-            jax.ShapeDtypeStruct((count, 8, tw), f32),
+            jax.ShapeDtypeStruct((groups, own_taps), f32),
         ),
         in_specs=[pl.BlockSpec(memory_space=pltpu.VMEM)] * 8,
         out_specs=(pl.BlockSpec(memory_space=pltpu.VMEM),) * 3,
@@ -302,24 +352,26 @@
             pltpu.VMEM((big // C, C, BAND), bf16),
             pltpu.VMEM((C, BAND), f32),
             pltpu.VMEM((count, 8, tw), f32),
+            pltpu.VMEM((count, 8, tw), f32),
+            pltpu.VMEM((8, tw), f32),
+            pltpu.VMEM((tps, 8, own_taps), f32),
+            pltpu.VMEM((tps, 8, own_taps), f32),
+            pltpu.VMEM((tps, 8, own_taps), f32),
             dma((count - 1,)), dma((count - 1,)),
             dma((chunks, 2)), dma((chunks, 2)),
             dma((2, 4 * chunks)), dma((2, 4 * chunks)),
             dma((chunks, 2)), dma((chunks, 2)),
             dma((count - 1,)), dma((count - 1,)),
+            dma((tps - 1,)), dma((tps - 1,)),
+            dma((tps - 1,)), dma((tps - 1,)),
         ],
         compiler_params=pltpu.CompilerParams(
             collective_id=0, has_side_effects=True, vmem_limit_bytes=58 * 1024 * 1024
         ),
-    )(taps, ids_col, ids_src, ids_grd, query_in, key_in, value_in, out_grad)
-
-    sender = lax.rem(here + count - jnp.arange(count), count)
-    odd = (sender % 2 == 1)[:, None]
-    each = diag[:, 0, ::-1]
+    )(taps_tp, ids_col, ids_src, ids_grd, query_in, key_in, value_in, out_grad)
+
     scale = 1.0 / math.sqrt(FGROUP * count * rows)
-    parts = jnp.stack([jnp.where(odd, 0.0, each).sum(0), jnp.where(odd, each, 0.0).sum(0)])
-    scaled = parts.reshape(held, 2 // held, tw).sum(1).T * scale
-    filter_grad = lax.all_to_all(scaled, "tp", split_axis=0, concat_axis=1, tiled=True)
+    filter_grad = sums[:, ::-1].T * scale
 
     skip = skip_gain[None, :]
     key_f, value_f = key_in.astype(f32), value_in.astype(f32)

time: 93.6 us -> 87.7 us (0.937)
  starting transfers between devices: 7.65 us -> 0 us
  Pallas kernels: 70.5 us -> 75.5 us
  local copies, waits for them, and re-layouts: 5.02 us -> 2.57 us
  waiting for transfers between devices: 1.21 us -> 0 us
    all_to_all x2 -> x0, starting transfers between devices: 7.65 us -> none  [the longest x1 4.25 us: shards(): lax.all_to_all(filter_taps, 'tp', split_axis=1, concat_axis=0, tiled=True)]
    pallas_call x1, Pallas kernels: 70.5 us -> 75.5 us  [shards(): pl.pallas_call(functools.partial(pair_kernel, half), out_shape=(jax.Shape...]
    unnamed x10 -> x8, local copies, waits for them, and re-layouts: 1.35 us -> 0.01 us
    all_to_all x2 -> x0, waiting for transfers between devices: 1.21 us -> none  [the longest x1 1.21 us: shards(): lax.all_to_all(filter_taps, 'tp', split_axis=1, concat_axis=0, tiled=True)]
  transfers between devices with their start and end apart: 2 -> 0, of which waited for: 1 -> 0; matrix products, arithmetic and copies ran while one was open for 9% -> 0% of each run, Pallas kernels for 0% -> 0%
where the time goes in v3:
time: 87.7 us; the launch traced here: 87.4 us
  Pallas kernels  75.5 us (86%)
  other arithmetic  8.67 us (10%)
  local copies, waits for them, and re-layouts  2.57 us (3%)
    pallas_call x1, Pallas kernels, shards(): pl.pallas_call(functools.partial(pair_kernel, half), out_shape=(jax.Shape...  75.5 us
    convert_element_type x1, other arithmetic, shards(): (mgrad * key_f).astype(bf16)  5.99 us

profile of v3, /device:TPU:0, one launch (start us, length us, event | category | flops | bytes accessed | tf_op | source)
XLA Modules:
  0.0 87.4 jit_solution(15492230158128221151)
XLA Ops:
  0.7 0.1 pad.5.clone
  0.7 0.7 reshape_reshape.9
  1.4 0.1 rev.6
  1.5 0.7 maximum_maximum_fusion.taps_tp
  2.2 0.7 fusion.11
  2.9 0.6 fusion.12
  3.5 1.0 %copy.12.ids_col = s32[1024,1]{1,0:T(8,128)} copy(s32[1024,1]{0,1:T(1,128)S(1)} %bitcast.12) | data formatting | bytes 8192 | tf_op jit(solution)/shard_map/reshape | solution.py:326
  4.6 0.0 copy-start
  4.6 0.0 copy-start.1
  4.6 0.0 copy-start.2
  4.6 0.0 copy-start.3
  4.6 75.5 %shard_map.110 = (bf16[512,1024]{1,0:T(8,128)(2,1)}, bf16[512,1024]{1,0:T(8,128)(2,1)}, f32[8,64]{1,0:T(8,128)}) custom-call(f32[4,8,64]{2,1,0:T(8,128)} %maximum_maximum_fusion.taps_tp, s32[1024,1]{1,0:T(8,128)} %copy.12.ids_col, s32[1,3072]{1,0:T(1,128)} %bitcast.9, s32[1,3072]{1,0:T(1,128)} %bitcast.8, bf16[512,1024]{1,0:T(8,128)(2,1)} %query.1, ...), custom_call_target="tpu_custom_call" | custom-call | tf_op jit(solution)/shard_map/pallas_call | solution.py:329
  80.1 0.7 rev.7
  80.8 0.6 multiply_bitcast_fusion
  81.4 0.0 copy-done
  81.4 0.0 copy-done.1
  81.4 0.0 copy-done.2
  81.4 0.0 copy-done.3
  81.4 6.0 %fusion.1 = (bf16[512,1024]{1,0:T(8,128)(2,1)}, bf16[512,1024]{1,0:T(8,128)(2,1)}, bf16[512,1024]{1,0:T(8,128)(2,1)}, bf16[512,1024]{1,0:T(8,128)(2,1)}) fusion(bf16[512,1024]{1,0:T(8,128)(2,1)S(1)} %copy-done, bf16[512,1024]{1,0:T(8,128)(2,1)} %get-tuple-element.9, bf16[512,1024]{1,0:T(8,128)(2,1)S(1)} %copy-done.1, bf16[512,1024]{1,0:T(8,128)(2,1)} %ograd.1, ...), kind=kLoop, calls=%fused_computation.7 | loop fusion | flops 11534336 | bytes 10489856 | tf_op jit(solution)/shard_map/convert_element_type | solution.py:385
  (3 shorter events, 0.0 us)
Async XLA Ops:
  4.6 76.9 %copy-start = (bf16[512,1024]{1,0:T(8,128)(2,1)S(1)}, bf16[512,1024]{1,0:T(8,128)(2,1)}, u32[]{:S(2)}) copy-start(bf16[512,1024]{1,0:T(8,128)(2,1)} %key.1) | copy-start | bytes 3145732
  4.6 76.9 %copy-start.1 = (bf16[512,1024]{1,0:T(8,128)(2,1)S(1)}, bf16[512,1024]{1,0:T(8,128)(2,1)}, u32[]{:S(2)}) copy-start(bf16[512,1024]{1,0:T(8,128)(2,1)} %query.1) | copy-start | bytes 3145732
  4.6 76.9 %copy-start.2 = (bf16[512,1024]{1,0:T(8,128)(2,1)S(1)}, bf16[512,1024]{1,0:T(8,128)(2,1)}, u32[]{:S(2)}) copy-start(bf16[512,1024]{1,0:T(8,128)(2,1)} %value.1) | copy-start | bytes 3145732
  4.6 76.9 %copy-start.3 = (f32[1024]{0:T(1024)S(1)}, f32[1024]{0:T(1024)}, u32[]{:S(2)}) copy-start(f32[1024]{0:T(1024)} %param.12) | copy-start | bytes 12292

commit v4 on v3

--- a/solution.py
+++ b/solution.py
@@ -30,7 +30,7 @@
     half, taps_tp, ids_col, ids_src, ids_grd, query, key, value, ograd,
     conv_out, back_out, sums_out,
     src, grd, give_m, give_g, conv_s, back_s, got_c, got_b,
-    taps_all, row_f, row_b, wide, wf, wb, acc, diag_send, diag_in, taps, taps_in, sums_send, sums_in,
+    taps_all, row_f, row_b, wide, wf, wb, acc, conv_near, back_near, diag_send, diag_in, taps, taps_in, sums_send, sums_in,
     t_send, t_recv, x_send, x_recv, z_send, z_recv, o_send, o_recv, d_send, d_recv, a_send, a_recv, b_send, b_recv,
 ):
     count = lax.axis_size("ctx")
@@ -204,18 +204,35 @@
     masked(row_b, 0, ids_grd, wb)
     acc[...] = jnp.zeros_like(acc)
 
-    def compute(c, first, end):
+    split = big + C
+
+    def near(c):
         def one(i, carry):
             row = pl.multiple_of(i * C, C)
-            own, span = pl.ds(row, C), pl.ds(row, BAND)
+            own, span = pl.ds(row, C), pl.ds(row + big, BAND - big)
             source = src[c, span, :]
-            conv_s[c, own, :] = jnp.dot(wf[i], source, preferred_element_type=f32).astype(jnp.bfloat16)
+            conv_near[own, :] = jnp.dot(wf[i, :, big:], source, preferred_element_type=f32)
             prod = lax.dot_general(grd[c, own, :], source, (((1,), (1,)), ((), ())), preferred_element_type=f32)
-            acc[...] += jnp.where(ids_col[own, :] == ids_src[:, span], prod, 0.0)
-            back_s[c, own, :] = jnp.dot(wb[i], grd[c, span, :], preferred_element_type=f32).astype(jnp.bfloat16)
+            acc[:, big:] += jnp.where(ids_col[own, :] == ids_src[:, span], prod, 0.0)
+            back_near[own, :] = jnp.dot(wb[i, :, :split], grd[c, pl.ds(row, split), :], preferred_element_type=f32)
             return carry
 
-        lax.fori_loop(first, end, one, 0)
+        lax.fori_loop(0, big // C, one, 0)
+
+    def far(c):
+        def one(i, carry):
+            row = pl.multiple_of(i * C, C)
+            own, span = pl.ds(row, C), pl.ds(row, big)
+            source = src[c, span, :]
+            ahead = jnp.dot(wf[i, :, :big], source, preferred_element_type=f32)
+            conv_s[c, own, :] = (conv_near[own, :] + ahead).astype(jnp.bfloat16)
+            prod = lax.dot_general(grd[c, own, :], source, (((1,), (1,)), ((), ())), preferred_element_type=f32)
+            acc[:, :big] += jnp.where(ids_col[own, :] == ids_src[:, span], prod, 0.0)
+            behind = jnp.dot(wb[i, :, split:], grd[c, pl.ds(row + split, BAND - split), :], preferred_element_type=f32)
+            back_s[c, own, :] = (back_near[own, :] + behind).astype(jnp.bfloat16)
+            return carry
+
+        lax.fori_loop(0, big // C, one, 0)
 
     def out_copies(c):
         theirs = at(0, False)
@@ -234,14 +251,13 @@
         conv_out[:, cols] = got_c[c]
         back_out[:, cols] = got_b[c]
 
-    middle = big // C // 2
     for c in range(chunks):
         forward_first(c + 2)
+        near(c)
+        forward_second(c + 1)
         end_hop(c, 0, 1)
         end_hop(c, 1, 1)
-        compute(c, 0, middle)
-        forward_second(c + 1)
-        compute(c, middle, big // C)
+        far(c)
         for copy in out_copies(c):
             copy.start()
 
@@ -351,6 +367,8 @@
             pltpu.VMEM((big // C, C, BAND), bf16),
             pltpu.VMEM((big // C, C, BAND), bf16),
             pltpu.VMEM((C, BAND), f32),
+            pltpu.VMEM((big, cw), f32),
+            pltpu.VMEM((big, cw), f32),
             pltpu.VMEM((count, 8, tw), f32),
             pltpu.VMEM((count, 8, tw), f32),
             pltpu.VMEM((8, tw), f32),

time: 87.7 us -> 85.7 us (0.977)
  Pallas kernels: 75.5 us -> 73.5 us
    pallas_call x1, Pallas kernels: 75.5 us -> 73.5 us  [shards(): pl.pallas_call(functools.partial(pair_kernel, half), out_shape=(jax.Shape...]
where the time goes in v4:
time: 85.7 us; the launch traced here: 85.4 us
  Pallas kernels  73.5 us (86%)
  other arithmetic  8.67 us (10%)
  local copies, waits for them, and re-layouts  2.57 us (3%)
    pallas_call x1, Pallas kernels, shards(): pl.pallas_call(functools.partial(pair_kernel, half), out_shape=(jax.Shape...  73.5 us
    convert_element_type x1, other arithmetic, shards(): (mgrad * key_f).astype(bf16)  5.99 us

profile of v4, /device:TPU:0, one launch (start us, length us, event | category | flops | bytes accessed | tf_op | source)
XLA Modules:
  0.0 85.4 jit_solution(11395811143337126118)
XLA Ops:
  0.7 0.1 pad.5.clone
  0.7 0.7 reshape_reshape.9
  1.4 0.1 rev.6
  1.5 0.7 maximum_maximum_fusion.taps_tp
  2.2 0.7 fusion.11
  2.9 0.6 fusion.12
  3.5 1.0 %copy.12.ids_col = s32[1024,1]{1,0:T(8,128)} copy(s32[1024,1]{0,1:T(1,128)S(1)} %bitcast.12) | data formatting | bytes 8192 | tf_op jit(solution)/shard_map/reshape | solution.py:342
  4.6 0.0 copy-start
  4.6 0.0 copy-start.1
  4.6 0.0 copy-start.2
  4.6 0.0 copy-start.3
  4.6 73.5 %shard_map.110 = (bf16[512,1024]{1,0:T(8,128)(2,1)}, bf16[512,1024]{1,0:T(8,128)(2,1)}, f32[8,64]{1,0:T(8,128)}) custom-call(f32[4,8,64]{2,1,0:T(8,128)} %maximum_maximum_fusion.taps_tp, s32[1024,1]{1,0:T(8,128)} %copy.12.ids_col, s32[1,3072]{1,0:T(1,128)} %bitcast.9, s32[1,3072]{1,0:T(1,128)} %bitcast.8, bf16[512,1024]{1,0:T(8,128)(2,1)} %query.1, ...), custom_call_target="tpu_custom_call" | custom-call | tf_op jit(solution)/shard_map/pallas_call | solution.py:345
  78.1 0.7 rev.7
  78.8 0.6 multiply_bitcast_fusion
  79.4 0.0 copy-done
  79.4 0.0 copy-done.1
  79.4 0.0 copy-done.2
  79.4 0.0 copy-done.3
  79.4 6.0 %fusion.1 = (bf16[512,1024]{1,0:T(8,128)(2,1)}, bf16[512,1024]{1,0:T(8,128)(2,1)}, bf16[512,1024]{1,0:T(8,128)(2,1)}, bf16[512,1024]{1,0:T(8,128)(2,1)}) fusion(bf16[512,1024]{1,0:T(8,128)(2,1)S(1)} %copy-done, bf16[512,1024]{1,0:T(8,128)(2,1)} %get-tuple-element.9, bf16[512,1024]{1,0:T(8,128)(2,1)S(1)} %copy-done.1, bf16[512,1024]{1,0:T(8,128)(2,1)} %ograd.1, ...), kind=kLoop, calls=%fused_computation.7 | loop fusion | flops 11534336 | bytes 10489856 | tf_op jit(solution)/shard_map/convert_element_type | solution.py:403
  (3 shorter events, 0.0 us)
Async XLA Ops:
  4.6 74.8 %copy-start = (bf16[512,1024]{1,0:T(8,128)(2,1)S(1)}, bf16[512,1024]{1,0:T(8,128)(2,1)}, u32[]{:S(2)}) copy-start(bf16[512,1024]{1,0:T(8,128)(2,1)} %key.1) | copy-start | bytes 3145732
  4.6 74.8 %copy-start.1 = (bf16[512,1024]{1,0:T(8,128)(2,1)S(1)}, bf16[512,1024]{1,0:T(8,128)(2,1)}, u32[]{:S(2)}) copy-start(bf16[512,1024]{1,0:T(8,128)(2,1)} %query.1) | copy-start | bytes 3145732
  4.6 74.8 %copy-start.2 = (bf16[512,1024]{1,0:T(8,128)(2,1)S(1)}, bf16[512,1024]{1,0:T(8,128)(2,1)}, u32[]{:S(2)}) copy-start(bf16[512,1024]{1,0:T(8,128)(2,1)} %value.1) | copy-start | bytes 3145732
  4.6 74.8 %copy-start.3 = (f32[1024]{0:T(1024)S(1)}, f32[1024]{0:T(1024)}, u32[]{:S(2)}) copy-start(f32[1024]{0:T(1024)} %param.12) | copy-start | bytes 12292
